TPU v7x, 32 devices: a whole 2x2x4 slice. The times are simulated.
32 devices in a mesh: groups: 2 (over y), wide: 4 (over z), layer: 2 (over core), mp: 2 (over x).
Axes of the slice: x: 2, y: 2, z: 4, core: 2. Of those that a mesh axis runs over, the one named last changes fastest.
Arguments:
- acts: bfloat16 [2, 16384, 4096], P('layer', ('groups', 'wide'), 'mp'), parts along dimension 1, may hold values from -6 to 6
- grads: bfloat16 [2, 16384, 4096], P('layer', ('groups', 'wide'), 'mp'), parts along dimension 1, may hold values from -6 to 6
- projections: bfloat16 [2, 4096, 128], P('layer', 'mp'), may hold values from -0.09375 to 0.09375
- lengths: int32 [64], P(('groups', 'wide')), parts along dimension 0, may hold values from 1 to 256, as said below
- queries: bfloat16 [2, 1024, 4096], P('layer', ('groups', 'wide'), 'mp'), parts along dimension 1, may hold values from -0.0625 to 0.0625
- query_ids: int32 [1024], P(('groups', 'wide')), parts along dimension 0, may hold values from 0 to 511, each once
Outputs:
- scores: float32 [64, 512], P(('groups', 'wide')), parts along dimension 0
There are 2 independent parts, one for each index of `groups`. A program takes and returns all parts, laid end to end along the dimension named above; an argument that names none is the same for every part. Nothing has to cross between parts.
Inputs may be any that keep to these rules, and one draw needn't show every extreme that they name: The lengths of one index of wide's 8 examples sum to at most 2048, and to exactly 2048 on at least one index.
All inputs are finite; a program needn't handle non-finite values.
Results may differ from a plain program's by a relative error of at most 0.0029.
Values may be sent and summed in bfloat16 or wider, within the bound.
A program may use at most 64 MiB of HBM per device.

v0:
```python
import jax
import jax.numpy as jnp
from jax import lax
from jax.sharding import PartitionSpec as P


def per_device(acts, grads, projections, lengths, queries, query_ids):
    tok_rows = acts.shape[1]
    rank = projections.shape[2] // 2
    mp_count = lax.axis_size("mp")
    slice_rank = rank // mp_count
    ex_count = lengths.shape[0]
    proj_x = jnp.dot(acts[0], projections[0][:, :rank], preferred_element_type=jnp.float32)
    proj_g = jnp.dot(grads[0], projections[0][:, rank:], preferred_element_type=jnp.float32)
    joined = jnp.concatenate([proj_x, proj_g], axis=1)
    ends = jnp.cumsum(lengths)
    starts = ends - lengths
    summed = lax.psum(joined, "mp")
    whole_x = summed[:, :rank]
    first = rank + lax.axis_index("mp") * slice_rank
    mine_g = lax.dynamic_slice_in_dim(summed, first, slice_rank, 1)
    rows = jnp.arange(tok_rows, dtype=jnp.int32)
    member = ((rows[None, :] >= starts[:, None]) & (rows[None, :] < ends[:, None])).astype(
        jnp.float32
    )
    weighted = member[:, None, :] * jnp.transpose(mine_g)[None, :, :]
    sums = jnp.einsum("eat,tb->eab", weighted, whole_x, precision=lax.Precision.HIGHEST)
    sums = sums / jnp.sqrt(lengths.astype(jnp.float32))[:, None, None]
    sketch = sums.reshape(ex_count, slice_rank * rank).astype(jnp.bfloat16)
    q_count = query_ids.shape[0]
    all_queries = q_count * lax.axis_size("wide")
    empty = jnp.zeros((ex_count, all_queries), jnp.float32)
    part_scores = jnp.einsum(
        "ef,qf->eq",
        sketch,
        lax.all_gather(queries, "wide", axis=1, tiled=True)[0],
        preferred_element_type=jnp.float32,
    )
    partial_scores = empty.at[
        :, lax.all_gather(query_ids[None, :], "wide", axis=1, tiled=True)[0]
    ].add(part_scores)
    return lax.psum(partial_scores, ("layer", "mp"))


def solution(mesh):
    return jax.shard_map(
        per_device,
        mesh=mesh,
        in_specs=(
            P("layer", ("groups", "wide"), "mp"),
            P("layer", ("groups", "wide"), "mp"),
            P("layer", "mp", None),
            P(("groups", "wide")),
            P("layer", ("groups", "wide"), "mp"),
            P(("groups", "wide")),
        ),
        out_specs=P(("groups", "wide"), None),
        check_vma=False,
    )
```

profile of v0, /device:TPU:0, one launch (start us, length us, event | category | flops | bytes accessed | tf_op | source)
XLA Modules:
  0.0 99.5 jit_solution(14867890486204120962)
XLA Ops:
  7.4 0.0 copy-start.1
  7.4 0.0 all-reduce.2.cloned.1.call-start
  7.4 0.0 copy-start
  7.4 6.3 %fusion = f32[2048,64]{0,1:T(8,128)S(1)} fusion(bf16[1,2048,2048]{2,1,0:T(8,128)(2,1)} %param.7, bf16[2048,128]{1,0:T(8,128)(2,1)} %bitcast.27), kind=kOutput, calls=%fused_computation.1 | convolution fusion | flops 536870912 | bytes 9437184 | tf_op jit(solution)/shard_map/dot_general | solution.py:14
  13.7 0.0 copy-done.1
  13.7 0.0 copy-done
  13.7 0.0 copy-start.3
  13.7 0.0 copy-start.2
  13.7 2.7 %fusion.2 = f32[2048,64]{0,1:T(8,128)S(1)} fusion(bf16[1,2048,2048]{2,1,0:T(8,128)(2,1)S(1)} %copy-done, bf16[2048,128]{1,0:T(8,128)(2,1)S(1)} %bitcast.28), kind=kOutput, calls=%fused_computation.3 | convolution fusion | flops 536870912 | bytes 9437184 | tf_op jit(solution)/shard_map/dot_general | solution.py:13
  16.4 1.1 %pad_maximum_fusion = f32[2048,128]{0,1:T(8,128)} fusion(f32[2048,64]{0,1:T(8,128)S(1)} %fusion, f32[2048,64]{0,1:T(8,128)S(1)} %fusion.2), kind=kLoop, calls=%fused_computation.12 | loop fusion | flops 262144 | bytes 2097152 | tf_op jit(solution)/shard_map/concatenate | solution.py:15
  17.4 0.0 all-reduce.2.cloned.1.call-update
  17.5 0.0 all-gather.4.cloned.1.call-start
  17.5 0.5 all-gather.4.cloned.1.call-update
  18.0 0.0 copy-done.3
  18.1 0.2 reduce-window.8
  18.2 0.0 copy-done.2
  18.2 12.5 %all-gather.1 = s32[4,1,128]{2,1,0:T(1,128)S(1)} all-gather(s32[1,1,128]{2,1,0:T(1,128)S(1)} %bitcast.31), channel_id=2, replica_groups=mesh['groups'=2,'wide'=4,'layer'=2,'mp'=2] {'wide'}, dimensions={0}, use_global_device_ids=true | all-gather | bytes 2560 | tf_op jit(solution)/shard_map/all_gather | solution.py:40
  30.8 0.1 fusion.24
  30.9 29.5 %all-reduce.2.cloned.1.call-done = f32[2048,128]{0,1:T(8,128)} async-done(((f32[2048,128]{0,1:T(8,128)}), f32[2048,128]{0,1:T(8,128)}) %all-reduce.2.cloned.1.call-update) | async-done | bytes 1048592 | tf_op jit(solution)/shard_map/psum | solution.py:18
  60.4 1.0 dynamic-slice_bitcast_fusion
  61.4 2.8 %fusion.11 = bf16[8,32,64]{2,1,0:T(8,128)(2,1)S(1)} fusion(f32[32,2048]{1,0:T(8,128)S(1)} %dynamic-slice_bitcast_fusion, f32[8,2048]{1,0:T(8,128)S(1)} %fusion.24, f32[2048,128]{0,1:T(8,128)} %all-reduce.2.cloned.1.call-done, f32[8]{0:T(128)S(1)} %convert_sqrt_fusion), kind=kOutput, calls=%fused_computation.10 | convolution fusion | flops 403210240 | bytes 884768 | tf_op jit(solution)/shard_map/eat,tb->eab/dot_general | solution.py:27
  64.2 0.1 convert_element_type.19
  64.3 3.5 %all-gather.4.cloned.1.call-done = bf16[1,512,2048]{2,1,0:T(8,128)(2,1)} async-done(((bf16[1,128,2048]{2,1,0:T(8,128)(2,1)}), bf16[1,512,2048]{2,1,0:T(8,128)(2,1)}) %all-gather.4.cloned.1.call-update) | async-done | bytes 2097168 | tf_op jit(solution)/shard_map/all_gather | solution.py:36
  67.9 2.2 %fusion.14 = f32[512,8]{0,1:T(8,128)S(1)} fusion(bf16[8,2048]{1,0:T(8,128)(2,1)S(1)} %convert_element_type.19, bf16[1,512,2048]{2,1,0:T(8,128)(2,1)} %all-gather.4.cloned.1.call-done), kind=kOutput, calls=%fused_computation.11 | convolution fusion | flops 16777216 | bytes 2146304 | tf_op jit(solution)/shard_map/ef,qf->eq/dot_general | solution.py:33
  70.1 0.1 copy.9
  70.2 2.3 %scatter_custom_fusion = f32[8,512]{0,1:T(8,128)S(1)} fusion(s32[512]{0:T(512)S(1)} %bitcast.29, f32[512,8]{1,0:T(8,128)S(1)} %copy.9, f32[]{:T(128)} %constant.7.clone.1), kind=kCustom, calls=%fused_computation.19 | custom fusion | flops 4096 | bytes 16388 | tf_op jit(solution)/shard_map/scatter-add | solution.py:41
  72.6 18.7 %psum.15 = f32[8,512]{0,1:T(8,128)S(1)} all-reduce(f32[8,512]{0,1:T(8,128)S(1)} %scatter_custom_fusion), channel_id=1, replica_groups=mesh['groups'=2,'wide'=4,'layer'=2,'mp'=2] {'layer','mp'}, use_global_device_ids=true, to_apply=%region_3.4 | all-reduce | flops 4096 | bytes 32768 | tf_op jit(solution)/shard_map/psum | solution.py:42
  91.3 0.7 copy.10
  (3 shorter events, 0.0 us)
Async XLA Ops:
  7.4 6.3 %copy-start.1 = (bf16[1,2048,128]{2,1,0:T(8,128)(2,1)S(1)}, bf16[1,2048,128]{2,1,0:T(8,128)(2,1)}, u32[]{:S(2)}) copy-start(bf16[1,2048,128]{2,1,0:T(8,128)(2,1)} %param.8) | copy-start | bytes 1572868
  7.4 53.0 %all-reduce.2.cloned.1.call-start = ((), (), s32[]{:S(2)}) async-start(), calls=%async_computation | async-start | bytes 2097152 | tf_op jit(solution)/shard_map/psum | solution.py:18
  7.4 6.3 %copy-start = (bf16[1,2048,2048]{2,1,0:T(8,128)(2,1)S(1)}, bf16[1,2048,2048]{2,1,0:T(8,128)(2,1)}, u32[]{:S(2)}) copy-start(bf16[1,2048,2048]{2,1,0:T(8,128)(2,1)} %param.6) | copy-start | bytes 25165828
  13.7 4.4 %copy-start.3 = (s32[8]{0:T(128)S(1)}, s32[8]{0:T(128)}, u32[]{:S(2)}) copy-start(s32[8]{0:T(128)} %param.9) | copy-start | bytes 100
  13.7 4.5 %copy-start.2 = (s32[128]{0:T(128)S(1)}, s32[128]{0:T(128)}, u32[]{:S(2)}) copy-start(s32[128]{0:T(128)} %param.11) | copy-start | bytes 1540
  17.5 50.4 %all-gather.4.cloned.1.call-start = ((), (), s32[]{:S(2)}) async-start(), calls=%async_computation.1 | async-start | bytes 2621440 | tf_op jit(solution)/shard_map/all_gather | solution.py:36
Sparse Core Ops, SparseCore 0:
  17.6 42.7 all-reduce.1
Sparse Core Ops, SparseCore 1:
  19.6 48.2 all-gather.3
where the time goes:
time: 99.7 us; the launch traced here: 99.5 us
  waiting for transfers between devices  33.6 us (34%)
  blocking collectives  31.3 us (31%)
  between operations  14.9 us (15%)
  matrix products  14 us (14%)
  other arithmetic  3.65 us (4%)
  local copies, waits for them, and re-layouts  1.97 us (2%)
    psum x1, waiting for transfers between devices, per_device(): summed = lax.psum(joined, 'mp')  29.5 us
    psum x1, blocking collectives, per_device(): return lax.psum(partial_scores, ('layer', 'mp'))  18.7 us
    all_gather x1, blocking collectives, per_device(): lax.all_gather(query_ids[None, :], 'wide', axis=1, tiled=True)[0]  12.5 us
    dot_general x1, matrix products, per_device(): jnp.dot(grads[0], projections[0][:, rank:], preferred_element_type=jnp.fl...  6.3 us
    all_gather x1, waiting for transfers between devices, per_device(): lax.all_gather(queries, 'wide', axis=1, tiled=True)[0]  3.53 us
    dot_general x1, matrix products, per_device(): jnp.einsum('eat,tb->eab', weighted, whole_x, precision=lax.Precision.HIGH...  2.82 us
    dot_general x1, matrix products, per_device(): jnp.dot(acts[0], projections[0][:, :rank], preferred_element_type=jnp.flo...  2.66 us
    scatter-add x1, other arithmetic, per_device(): partial_scores = empty.at[:, lax.all_gather(query_ids[None, :], 'wide', a...  2.32 us
  transfers between devices with their start and end apart: 2, of which 2 were waited for; matrix products, arithmetic and copies ran while one was open for 4% of the time, Pallas kernels for 0%

commit v1 on v0

v1 whole, which is shorter than its diff:
```python
import functools

import jax
import jax.numpy as jnp
from jax import lax
from jax.experimental import pallas as pl
from jax.experimental.pallas import tpu as pltpu
from jax.sharding import PartitionSpec as P

MESH = pl.DeviceIdType.MESH
F32 = jnp.float32
BF16 = jnp.bfloat16
NT = (((1,), (1,)), ((), ()))


def each(first, last, body):
    if last - first <= 16:
        for i in range(first, last):
            body(i)
    else:
        pl.loop(first, last)(body)


def kernel(
    sizes, acts, grads, proj, lens, queries, ids, out,
    a_buf, g_buf, w_buf, wx_buf, q_buf, id_buf, len_buf,
    g_own, g_send, g_recv, acc, part, part_recv, s_send, s_recv,
    sc_send, sc_recv, onehot,
    in_sem, a_sem, gr_sem, g_ssem, g_rsem, p_ssem, p_rsem,
    s_ssem, s_rsem, id_ssem, id_rsem, sc_ssem, sc_rsem,
):
    W, L, M = sizes
    N = W * L * M
    w = lax.axis_index("wide")
    l = lax.axis_index("layer")
    m = lax.axis_index("mp")
    me = (w * L + l) * M + m
    n_chunk, C, _ = a_buf.shape
    rank = w_buf.shape[1] // 2
    ex = len_buf.shape[0]
    mine_pairs = part_recv.shape[1]

    def local(src, dst, sem):
        return pltpu.make_async_copy(src, dst, sem)

    def rows(c):
        return pl.ds(pl.multiple_of(c * C, C), C)

    local(proj.at[0], w_buf, in_sem.at[0]).start()
    local(lens, len_buf, in_sem.at[1]).start()
    for c in range(n_chunk):
        local(grads.at[0, rows(c)], g_buf.at[c], gr_sem.at[c]).start()
    for c in range(n_chunk):
        local(acts.at[0, rows(c)], a_buf.at[c], a_sem.at[c]).start()
    local(ids, id_buf.at[w], in_sem.at[2]).start()
    local(queries.at[0], q_buf, in_sem.at[3]).start()

    barrier = pltpu.get_barrier_semaphore()

    def place(d):
        other = lax.rem(me + d, N)
        return other // (L * M), (other // M) % L, other % M

    def greet(d):
        ow, ol, om = place(d)
        pl.semaphore_signal(
            barrier, inc=1, device_id={"wide": ow, "layer": ol, "mp": om}, device_id_type=MESH
        )

    each(1, N, greet)

    sub = lax.broadcasted_iota(jnp.int32, (ex, C), 0)
    lane = lax.broadcasted_iota(jnp.int32, (ex, C), 1)
    local(lens, len_buf, in_sem.at[1]).wait()
    first = jnp.zeros((ex, C), jnp.int32)
    last = jnp.zeros((ex, C), jnp.int32)
    run = jnp.int32(0)
    for e in range(ex):
        first = jnp.where(sub == e, run, first)
        run = run + len_buf[e]
        last = jnp.where(sub == e, run, last)

    acc[...] = jnp.zeros_like(acc)
    local(proj.at[0], w_buf, in_sem.at[0]).wait()
    wx = w_buf[:, :rank]
    wx_buf[...] = jnp.concatenate([wx, wx], axis=1)

    def g_copy(d, c):
        to = lax.rem(m + d, M)
        return pltpu.make_async_remote_copy(
            src_ref=g_send.at[c],
            dst_ref=g_recv.at[d - 1, c],
            send_sem=g_ssem.at[d - 1, c],
            recv_sem=g_rsem.at[d - 1, c],
            device_id={"mp": to},
            device_id_type=MESH,
        )

    def project_g(c):
        local(grads.at[0, rows(c)], g_buf.at[c], gr_sem.at[c]).wait()
        g = jnp.dot(g_buf[c], w_buf[...], preferred_element_type=F32)
        gt = jnp.transpose(g)[rank:, :]
        g_own[c] = gt
        g_send[c] = gt.astype(BF16)

    project_g(0)
    pl.semaphore_wait(barrier, N - 1)
    for d in range(1, M):
        g_copy(d, 0).start()

    @pl.loop(1, n_chunk)
    def _(c):
        project_g(c)
        for d in range(1, M):
            g_copy(d, c).start()

    local(ids, id_buf.at[w], in_sem.at[2]).wait()

    def id_copy(d):
        return pltpu.make_async_remote_copy(
            src_ref=id_buf.at[w],
            dst_ref=id_buf.at[w],
            send_sem=id_ssem.at[d - 1],
            recv_sem=id_rsem.at[d - 1],
            device_id={"wide": lax.rem(w + d, W)},
            device_id_type=MESH,
        )

    for d in range(1, W):
        id_copy(d).start()

    @pl.loop(0, n_chunk)
    def _(c):
        local(acts.at[0, rows(c)], a_buf.at[c], a_sem.at[c]).wait()
        x = jnp.dot(a_buf[c], wx_buf[...], preferred_element_type=F32)
        x_hi = x.astype(BF16)
        x_lo = (x - x_hi.astype(F32)).astype(BF16)
        right = jnp.concatenate([x_hi, x_lo], axis=1)
        g = g_own[c]
        for d in range(1, M):
            g_copy(d, c).wait_recv()
            g = g + g_recv[d - 1, c].astype(F32)
        g_hi = g.astype(BF16).astype(F32)
        g_lo = g - g_hi
        t = lane + c * C
        member = (t >= first) & (t < last)
        for i, side in enumerate((g_hi, g_lo)):
            left = jnp.concatenate(
                [
                    jnp.where(member, jnp.broadcast_to(side[a : a + 1, :], (ex, C)), 0.0)
                    for a in range(rank)
                ],
                axis=0,
            ).astype(BF16)
            acc[i] += jnp.dot(left, right, preferred_element_type=F32)

    wide_lane = lax.broadcasted_iota(jnp.int32, (rank // 2, ex, 2 * rank), 2)
    sums = acc[0, :, : 2 * rank] + acc[0, :, 2 * rank :] + acc[1, :, : 2 * rank]
    sums = sums.reshape(rank // 2, 2, ex, 2 * rank)
    part[...] = jnp.where(wide_lane < rank, sums[:, 0], sums[:, 1])

    def p_copy(d):
        to = lax.rem(m + d, M)
        return pltpu.make_async_remote_copy(
            src_ref=part.at[pl.ds(to * mine_pairs, mine_pairs)],
            dst_ref=part_recv.at[d - 1],
            send_sem=p_ssem.at[d - 1],
            recv_sem=p_rsem.at[d - 1],
            device_id={"mp": to},
            device_id_type=MESH,
        )

    for d in range(1, M):
        p_copy(d).start()

    root = jnp.zeros((ex, 2 * rank), jnp.int32)
    for e in range(ex):
        root = jnp.where(sub[:, : 2 * rank] == e, len_buf[e], root)
    root = jnp.sqrt(root.astype(F32))

    for d in range(1, W):
        id_copy(d).wait()
    q_rows = id_buf.shape[2]
    for v in range(W):
        number = lax.broadcasted_iota(jnp.int32, (W * q_rows, q_rows), 0)
        onehot[:, v * q_rows : (v + 1) * q_rows] = jnp.where(
            number == id_buf[v], 1.0, 0.0
        ).astype(BF16)
    local(queries.at[0], q_buf, in_sem.at[3]).wait()

    total = part[pl.ds(m * mine_pairs, mine_pairs)]
    for d in range(1, M):
        p_copy(d).wait_recv()
        total = total + part_recv[d - 1]
    sketch = total / root[None]
    s_send[...] = sketch.reshape(mine_pairs * ex, 2 * rank).astype(BF16)

    def s_copy(d):
        return pltpu.make_async_remote_copy(
            src_ref=s_send,
            dst_ref=s_recv.at[d - 1],
            send_sem=s_ssem.at[d - 1],
            recv_sem=s_rsem.at[d - 1],
            device_id={"wide": lax.rem(w + d, W)},
            device_id_type=MESH,
        )

    for d in range(1, W):
        s_copy(d).start()

    def score(block):
        block = block.astype(F32).reshape(mine_pairs, ex, 2 * rank)
        left = jnp.concatenate([block[k] for k in range(mine_pairs)], axis=1).astype(BF16)
        return lax.dot_general(left, q_buf[...], NT, preferred_element_type=F32)

    def sc_copy(ow, lm):
        other = lax.rem(l * M + m + lm, L * M)
        slot = (lax.rem(ow - w + W, W)) * (L * M) + lm
        return pltpu.make_async_remote_copy(
            src_ref=sc_send.at[ow],
            dst_ref=sc_recv.at[w, lm],
            send_sem=sc_ssem.at[slot],
            recv_sem=sc_rsem.at[w, lm],
            device_id={"wide": ow, "layer": other // M, "mp": other % M},
            device_id_type=MESH,
        )

    own = score(s_send[...])
    sc_send[w] = own
    for lm in range(1, L * M):
        sc_copy(w, lm).start()
    for d in range(1, W):
        s_copy(d).wait_recv()
        ow = lax.rem(w - d + W, W)
        sc_send[ow] = score(s_recv[d - 1])
        for lm in range(L * M):
            sc_copy(ow, lm).start()

    sc_recv[w, 0] = own

    def arrive(v, lm):
        sc = sc_recv.at[v, lm]
        pltpu.make_async_copy(sc, sc, sc_rsem.at[v, lm]).wait()

    for lm in range(1, L * M):
        arrive(w, lm)
    for d in range(1, W):
        v = lax.rem(w + d, W)
        for lm in range(L * M):
            arrive(v, lm)
    blocks = []
    for v in range(W):
        block = sc_recv[v, 0]
        for lm in range(1, L * M):
            block = block + sc_recv[v, lm]
        blocks.append(block)
    scores = jnp.concatenate(blocks, axis=1)
    high = scores.astype(BF16).astype(F32)
    rest = scores - high
    middle = rest.astype(BF16).astype(F32)
    low = rest - middle
    pieces = jnp.concatenate([high, middle, low, jnp.zeros_like(low)], axis=0).astype(BF16)
    placed = lax.dot_general(pieces, onehot[...], NT, preferred_element_type=F32)
    out[...] = placed[:ex] + placed[ex : 2 * ex] + placed[2 * ex : 3 * ex]

    for d in range(1, M):
        p_copy(d).wait_send()
        for c in range(n_chunk):
            g_copy(d, c).wait_send()
    for d in range(1, W):
        s_copy(d).wait_send()
    for d in range(W):
        ow = lax.rem(w - d + W, W)
        for lm in range(1 if d == 0 else 0, L * M):
            sc_copy(ow, lm).wait_send()


def per_device(acts, grads, projections, lengths, queries, query_ids):
    W, L, M = (lax.axis_size(name) for name in ("wide", "layer", "mp"))
    _, tokens, depth = acts.shape
    rank2 = projections.shape[2]
    rank = rank2 // 2
    ex = lengths.shape[0]
    q_rows = queries.shape[1]
    C = 256
    n_chunk = tokens // C
    mine_pairs = rank // 2 // M
    dma = pltpu.SemaphoreType.DMA
    moves = tokens * depth * 4 + depth * rank2 * 2 + q_rows * depth * 2
    return pl.pallas_call(
        functools.partial(kernel, (W, L, M)),
        out_shape=jax.ShapeDtypeStruct((ex, q_rows * W), F32),
        in_specs=[pl.BlockSpec(memory_space=pl.ANY)] * 6,
        out_specs=pl.BlockSpec(memory_space=pltpu.VMEM),
        scratch_shapes=[
            pltpu.VMEM((n_chunk, C, depth), BF16),
            pltpu.VMEM((n_chunk, C, depth), BF16),
            pltpu.VMEM((depth, rank2), BF16),
            pltpu.VMEM((depth, rank2), BF16),
            pltpu.VMEM((q_rows, depth), BF16),
            pltpu.VMEM((W, 1, q_rows), jnp.int32),
            pltpu.SMEM((ex,), jnp.int32),
            pltpu.VMEM((n_chunk, rank, C), F32),
            pltpu.VMEM((n_chunk, rank, C), BF16),
            pltpu.VMEM((max(M - 1, 1), n_chunk, rank, C), BF16),
            pltpu.VMEM((2, rank * ex, 2 * rank2), F32),
            pltpu.VMEM((rank // 2, ex, rank2), F32),
            pltpu.VMEM((max(M - 1, 1), mine_pairs, ex, rank2), F32),
            pltpu.VMEM((mine_pairs * ex, rank2), BF16),
            pltpu.VMEM((max(W - 1, 1), mine_pairs * ex, rank2), BF16),
            pltpu.VMEM((W, ex, q_rows), F32),
            pltpu.VMEM((W, L * M, ex, q_rows), F32),
            pltpu.VMEM((q_rows * W, q_rows * W), BF16),
            dma((4,)),
            dma((n_chunk,)),
            dma((n_chunk,)),
            dma((max(M - 1, 1), n_chunk)),
            dma((max(M - 1, 1), n_chunk)),
            dma((max(M - 1, 1),)),
            dma((max(M - 1, 1),)),
            dma((max(W - 1, 1),)),
            dma((max(W - 1, 1),)),
            dma((max(W - 1, 1),)),
            dma((max(W - 1, 1),)),
            dma((W * L * M,)),
            dma((W, L * M)),
        ],
        compiler_params=pltpu.CompilerParams(
            collective_id=0, has_side_effects=True, vmem_limit_bytes=56 * 1024 * 1024
        ),
        cost_estimate=pl.CostEstimate(
            flops=tokens * depth * rank2 * 4, bytes_accessed=moves, transcendentals=0
        ),
    )(acts, grads, projections, lengths, queries, query_ids.reshape(1, q_rows))


def solution(mesh):
    return jax.shard_map(
        per_device,
        mesh=mesh,
        in_specs=(
            P("layer", ("groups", "wide"), "mp"),
            P("layer", ("groups", "wide"), "mp"),
            P("layer", "mp", None),
            P(("groups", "wide")),
            P("layer", ("groups", "wide"), "mp"),
            P(("groups", "wide")),
        ),
        out_specs=P(("groups", "wide"), None),
        check_vma=False,
    )
```

time: 99.7 us -> 31.8 us (0.32)
  waiting for transfers between devices: 33.6 us -> 0 us
  blocking collectives: 31.3 us -> 0 us
  Pallas kernels: 0 us -> 30.2 us
  between operations: 14.9 us -> 0.01 us
  matrix products: 14 us -> 0 us
  other arithmetic: 3.65 us -> 0 us
    pallas_call x0 -> x1, Pallas kernels: none -> 30.2 us  [per_device(): pl.pallas_call(functools.partial(kernel, (W, L, M)), out_shape=jax.ShapeD...]
    psum x1 -> x0, waiting for transfers between devices: 29.5 us -> none  [per_device(): summed = lax.psum(joined, 'mp')]
    psum x1 -> x0, blocking collectives: 18.7 us -> none  [per_device(): return lax.psum(partial_scores, ('layer', 'mp'))]
    dot_general x4 -> x0, matrix products: 14 us -> none  [the longest x1 6.3 us: per_device(): jnp.dot(grads[0], projections[0][:, rank:], preferred_element_type=jnp.fl...]
    all_gather x1 -> x0, blocking collectives: 12.5 us -> none  [per_device(): lax.all_gather(query_ids[None, :], 'wide', axis=1, tiled=True)[0]]
    all_gather x1 -> x0, waiting for transfers between devices: 3.53 us -> none  [per_device(): lax.all_gather(queries, 'wide', axis=1, tiled=True)[0]]
    scatter-add x1 -> x0, other arithmetic: 2.32 us -> none  [per_device(): partial_scores = empty.at[:, lax.all_gather(query_ids[None, :], 'wide', a...]
    unnamed x8 -> x1, local copies, waits for them, and re-layouts: 0.02 us -> 1.32 us
  transfers between devices with their start and end apart: 2 -> 0, of which waited for: 2 -> 0; matrix products, arithmetic and copies ran while one was open for 4% -> 0% of each run, Pallas kernels for 0% -> 0%
where the time goes in v1:
time: 31.8 us; the launch traced here: 31.6 us
  Pallas kernels  30.2 us (95%)
  local copies, waits for them, and re-layouts  1.32 us (4%)
    pallas_call x1, Pallas kernels, per_device(): pl.pallas_call(functools.partial(kernel, (W, L, M)), out_shape=jax.ShapeD...  30.2 us
    unnamed x1, local copies, waits for them, and re-layouts  1.32 us

profile of v1, /device:TPU:0, one launch (start us, length us, event | category | flops | bytes accessed | tf_op | source)
XLA Modules:
  0.0 31.6 jit_solution(16636755606235412521)
XLA Ops:
  0.0 30.2 %shard_map.64 = f32[8,512]{1,0:T(8,128)} custom-call(bf16[1,2048,2048]{2,1,0:T(8,128)(2,1)} %acts.1, bf16[1,2048,2048]{2,1,0:T(8,128)(2,1)} %grads.1, bf16[1,2048,128]{2,1,0:T(8,128)(2,1)} %proj.1, s32[8]{0:T(128)} %lens.1, bf16[1,128,2048]{2,1,0:T(8,128)(2,1)} %queries.1, s32[1,128]{1,0:T(1,128)} %bitcast.1), custom_call_target="tpu_custom_call" | custom-call | flops 2147483648 | bytes 17825792 | tf_op jit(solution)/shard_map/pallas_call | solution.py:290
  30.2 1.3 %copy.8 = f32[8,512]{1,0:T(8,128)} copy(f32[8,512]{1,0:T(8,128)} %shard_map.64) | data formatting | bytes 32768

commit v2 on v1

--- a/solution.py
+++ b/solution.py
@@ -282,7 +282,7 @@
     rank = rank2 // 2
     ex = lengths.shape[0]
     q_rows = queries.shape[1]
-    C = 256
+    C = 512
     n_chunk = tokens // C
     mine_pairs = rank // 2 // M
     dma = pltpu.SemaphoreType.DMA

time: 31.8 us -> 31.1 us (0.978)
  Pallas kernels: 30.2 us -> 29.6 us
    pallas_call x1, Pallas kernels: 30.2 us -> 29.6 us  [per_device(): pl.pallas_call(functools.partial(kernel, (W, L, M)), out_shape=jax.ShapeD...]
where the time goes in v2:
time: 31.1 us; the launch traced here: 30.9 us
  Pallas kernels  29.6 us (95%)
  local copies, waits for them, and re-layouts  1.32 us (4%)
    pallas_call x1, Pallas kernels, per_device(): pl.pallas_call(functools.partial(kernel, (W, L, M)), out_shape=jax.ShapeD...  29.6 us
    unnamed x1, local copies, waits for them, and re-layouts  1.32 us

profile of v2, /device:TPU:0, one launch (start us, length us, event | category | flops | bytes accessed | tf_op | source)
XLA Modules:
  0.0 30.9 jit_solution(1217460192675350529)
XLA Ops:
  0.0 29.6 %shard_map.64 = f32[8,512]{1,0:T(8,128)} custom-call(bf16[1,2048,2048]{2,1,0:T(8,128)(2,1)} %acts.1, bf16[1,2048,2048]{2,1,0:T(8,128)(2,1)} %grads.1, bf16[1,2048,128]{2,1,0:T(8,128)(2,1)} %proj.1, s32[8]{0:T(128)} %lens.1, bf16[1,128,2048]{2,1,0:T(8,128)(2,1)} %queries.1, s32[1,128]{1,0:T(1,128)} %bitcast.1), custom_call_target="tpu_custom_call" | custom-call | flops 2147483648 | bytes 17825792 | tf_op jit(solution)/shard_map/pallas_call | solution.py:290
  29.6 1.3 %copy.8 = f32[8,512]{1,0:T(8,128)} copy(f32[8,512]{1,0:T(8,128)} %shard_map.64) | data formatting | bytes 32768

commit v3 on v2

--- a/solution.py
+++ b/solution.py
@@ -80,7 +80,6 @@
         run = run + len_buf[e]
         last = jnp.where(sub == e, run, last)
 
-    acc[...] = jnp.zeros_like(acc)
     local(proj.at[0], w_buf, in_sem.at[0]).wait()
     wx = w_buf[:, :rank]
     wx_buf[...] = jnp.concatenate([wx, wx], axis=1)
@@ -104,6 +103,7 @@
         g_send[c] = gt.astype(BF16)
 
     project_g(0)
+    acc[...] = jnp.zeros_like(acc)
     pl.semaphore_wait(barrier, N - 1)
     for d in range(1, M):
         g_copy(d, 0).start()
@@ -154,10 +154,13 @@
             ).astype(BF16)
             acc[i] += jnp.dot(left, right, preferred_element_type=F32)
 
-    wide_lane = lax.broadcasted_iota(jnp.int32, (rank // 2, ex, 2 * rank), 2)
-    sums = acc[0, :, : 2 * rank] + acc[0, :, 2 * rank :] + acc[1, :, : 2 * rank]
-    sums = sums.reshape(rank // 2, 2, ex, 2 * rank)
-    part[...] = jnp.where(wide_lane < rank, sums[:, 0], sums[:, 1])
+    wide_lane = lax.broadcasted_iota(jnp.int32, (mine_pairs, ex, 2 * rank), 2)
+
+    def partial(j):
+        at = pl.ds(pl.multiple_of(j * (2 * mine_pairs * ex), 2 * mine_pairs * ex), 2 * mine_pairs * ex)
+        sums = acc[0, at, : 2 * rank] + acc[0, at, 2 * rank :] + acc[1, at, : 2 * rank]
+        sums = sums.reshape(mine_pairs, 2, ex, 2 * rank)
+        return jnp.where(wide_lane < rank, sums[:, 0], sums[:, 1])
 
     def p_copy(d):
         to = lax.rem(m + d, M)
@@ -171,6 +174,8 @@
         )
 
     for d in range(1, M):
+        to = lax.rem(m + d, M)
+        part[pl.ds(to * mine_pairs, mine_pairs)] = partial(to)
         p_copy(d).start()
 
     root = jnp.zeros((ex, 2 * rank), jnp.int32)
@@ -188,7 +193,7 @@
         ).astype(BF16)
     local(queries.at[0], q_buf, in_sem.at[3]).wait()
 
-    total = part[pl.ds(m * mine_pairs, mine_pairs)]
+    total = partial(m)
     for d in range(1, M):
         p_copy(d).wait_recv()
         total = total + part_recv[d - 1]

time: 31.1 us -> 31.2 us (level)
  no operation moved by 1% of the time
where the time goes in v3:
time: 31.2 us; the launch traced here: 30.9 us
  Pallas kernels  29.6 us (95%)
  local copies, waits for them, and re-layouts  1.32 us (4%)
    pallas_call x1, Pallas kernels, per_device(): pl.pallas_call(functools.partial(kernel, (W, L, M)), out_shape=jax.ShapeD...  29.6 us
    unnamed x1, local copies, waits for them, and re-layouts  1.32 us

profile of v3, /device:TPU:0, one launch (start us, length us, event | category | flops | bytes accessed | tf_op | source)
XLA Modules:
  0.0 30.9 jit_solution(9209803295451356370)
XLA Ops:
  0.0 29.6 %shard_map.64 = f32[8,512]{1,0:T(8,128)} custom-call(bf16[1,2048,2048]{2,1,0:T(8,128)(2,1)} %acts.1, bf16[1,2048,2048]{2,1,0:T(8,128)(2,1)} %grads.1, bf16[1,2048,128]{2,1,0:T(8,128)(2,1)} %proj.1, s32[8]{0:T(128)} %lens.1, bf16[1,128,2048]{2,1,0:T(8,128)(2,1)} %queries.1, s32[1,128]{1,0:T(1,128)} %bitcast.1), custom_call_target="tpu_custom_call" | custom-call | flops 2147483648 | bytes 17825792 | tf_op jit(solution)/shard_map/pallas_call | solution.py:295
  29.6 1.3 %copy.8 = f32[8,512]{1,0:T(8,128)} copy(f32[8,512]{1,0:T(8,128)} %shard_map.64) | data formatting | bytes 32768
